TPU v7x, 256 devices: a whole 4x4x8 slice. The times are simulated.
256 devices in a mesh: dp: 16 (over y, x), shard: 16 (over z, core).
Axes of the slice: x: 4, y: 4, z: 8, core: 2. Of those that a mesh axis runs over, the one named last changes fastest.
Arguments:
- grad_parts: bfloat16 [16, 16, 1536, 1536], P('dp', None, 'shard'), may hold values from -48 to 48
- momentum_owned: float32 [16, 16, 96, 1536], P('shard', None, 'dp'), may hold values from -6 to 6
- owner_table: int32 [16], replicated, may hold values from 0 to 15, each once
- step_offset: int32 [1], replicated, may hold values from 0 to 15
Outputs:
- updates: bfloat16 [16, 1536, 1536], P('dp', 'shard')
- new_momentum: float32 [16, 16, 96, 1536], P('shard', None, 'dp')
Inputs may be any that keep to these rules, and one draw needn't show every extreme that they name: `owner_table`: each owner slot is named by exactly one matrix.
All inputs are finite; a program needn't handle non-finite values.
Results may differ from a plain program's by a relative error of at most 0.0089.
Values may be sent and summed in bfloat16 or wider, within the bound.
No kernel may reach another device: no remote copies, remote signals or barrier semaphores. Data moves between devices by JAX's collectives and lax.ppermute only.
A program may use at most 64 MiB of HBM per device.

v0:
```python
import jax
import jax.numpy as jnp
from jax import lax
from jax.experimental import pallas as pl
from jax.experimental.pallas import tpu as pltpu
from jax.sharding import PartitionSpec as P

D = 1536
ITERS = 2
TILE = 512

momentum_decay = 0.95
linear_coef = 3.4445
cubic_coef = -4.775
quintic_coef = 2.0315


def swap(value, axis):
    return lax.all_to_all(value, axis, split_axis=0, concat_axis=0, tiled=True)


def shift(value, axis, by):
    count = lax.axis_size(axis)
    return lax.ppermute(value, axis, [(i, (i + by) % count) for i in range(count)])


def core_swap(value):
    return lax.ppermute(value, "core", [(0, 1), (1, 0)])


def pick_blocks(blocks, order):
    return blocks.at[order].get(mode="promise_in_bounds")


def after(value, other):
    return lax.optimization_barrier((value, other))


def spread_sums(picks, axes):
    places = [lax.axis_index(axis) for axis in axes]
    counts = [lax.axis_size(axis) for axis in axes]
    target = [
        lambda by, pick=pick, place=place, count=count: pick(lax.rem(place + by, count))
        for pick, place, count in zip(picks, places, counts)
    ]
    near = [
        [shift(block(1), axis, 1), shift(block(count - 1), axis, -1)]
        for block, axis, count in zip(target, axes, counts)
    ]
    far = []
    for n, (block, axis) in enumerate(zip(target, axes)):
        sent = block(2)
        if n > 0:
            sent, near[n][0] = after(sent, near[n][0])
        far.append(shift(sent, axis, 2))
    totals = []
    for n, block in enumerate(target):
        total = block(0).astype(jnp.float32)
        for part in near[n] + [far[n]]:
            total = total + part.astype(jnp.float32)
        totals.append(total)
    return totals, near[-1][0]


def ring_gather(piece, axis):
    rows = piece.shape[0]
    forth, back = piece, piece
    pieces = [piece]
    for _ in range(lax.axis_size(axis) // 2 - 1):
        forth, back = shift(forth, axis, 1), shift(back, axis, -1)
        pieces += [forth, back]
    return pieces + [shift(forth[: rows // 2], axis, 1), shift(back[rows // 2 :], axis, -1)]


def newton_schulz_kernel(*refs):
    scratch = 8
    pieces, out_ref = refs[: -scratch - 1], refs[-scratch - 1]
    first_ref, later_ref, gram_ref, poly_ref, kept_ref, diag_ref, square_ref, sems = refs[-scratch:]
    tiles = D // TILE
    contract_last = (((1,), (1,)), ((), ()))
    copies, start = [], 0
    for n, piece in enumerate(pieces):
        height = piece.shape[0]
        copies.append(pltpu.make_async_copy(piece, first_ref.at[pl.ds(start, height), :], sems.at[n]))
        start += height
    for copy in copies:
        copy.start()
    diag_ref[...] = jnp.zeros_like(diag_ref)
    square_ref[...] = jnp.zeros_like(square_ref)
    for copy in copies:
        copy.wait()

    def span(start, size):
        return pl.ds(pl.multiple_of(start, 256), size)

    def symmetric(product, finish, target):
        def step(t, carry):
            i = (t >= 2).astype(jnp.int32) * TILE
            j = (1 + (t >= 1).astype(jnp.int32)) * TILE
            k = t * TILE
            small = TILE // 2
            for row, column, height, diagonal in (
                (i, j, TILE, False),
                (i, j + small, TILE, False),
                (k, k, TILE, True),
                (k + small, k + small, small, True),
            ):
                low = finish(row, column, height, diagonal, product(row, column, height))
                target[span(row, height), span(column, small)] = low
                if not diagonal:
                    target[span(column, small), span(row, height)] = low.T
                elif height == TILE:
                    target[span(column, small), span(row + small, small)] = low[small:, :].T
            return carry

        lax.fori_loop(0, tiles, step, 0)

    def sweep(source, store, measured):
        def gram_product(row, column, height):
            return lax.dot_general(
                source[span(row, height), :],
                source[span(column, TILE // 2), :],
                contract_last,
                preferred_element_type=jnp.float32,
            )

        def gram_finish(row, column, height, diagonal, total):
            if measured and diagonal:
                rows = lax.broadcasted_iota(jnp.int32, total.shape, 0)
                columns = lax.broadcasted_iota(jnp.int32, total.shape, 1)
                diag_ref[...] += jnp.sum(jnp.where(rows == columns, total, 0.0), axis=0, keepdims=True)
            return total.astype(jnp.bfloat16)

        symmetric(gram_product, gram_finish, gram_ref)
        if measured:
            inverse = 1.0 / (jnp.sqrt(jnp.sum(diag_ref[...])) + 1e-07)
            cubic = cubic_coef * (inverse * inverse)
            quintic = quintic_coef * (inverse * inverse) * (inverse * inverse)
        else:
            inverse, cubic, quintic = 1.0, cubic_coef, quintic_coef

        def poly_product(row, column, height):
            return jnp.dot(
                gram_ref[span(row, height), :], gram_ref[:, span(column, TILE // 2)], preferred_element_type=jnp.float32
            )

        def poly_finish(row, column, height, diagonal, total):
            gram = gram_ref[span(row, height), span(column, TILE // 2)].astype(jnp.float32)
            return (cubic * gram + quintic * total).astype(jnp.bfloat16)

        symmetric(poly_product, poly_finish, poly_ref)

        def mix_tile(t, carry):
            rows = span(t * TILE, TILE)
            for c in range(0, D, TILE // 2):
                columns = slice(c, c + TILE // 2)
                total = jnp.dot(poly_ref[rows, :], source[:, columns], preferred_element_type=jnp.float32)
                store(t, rows, columns, (linear_coef * source[rows, columns].astype(jnp.float32) + total) * inverse)
            return carry

        lax.fori_loop(0, tiles, mix_tile, 0)

    def store_later(t, rows, columns, mixed):
        later_ref[rows, columns] = mixed.astype(jnp.bfloat16)

    def store_mixed(t, rows, columns, mixed):
        kept_ref[t, :, columns] = mixed[: kept_ref.shape[1], :]
        square_ref[:, columns] += jnp.sum(mixed * mixed, axis=0, keepdims=True)

    sweep(first_ref, store_later, True)
    sweep(later_ref, store_mixed, False)
    scale = lax.rsqrt(jnp.sum(square_ref[...]) / (D * D) + 1e-06)
    out_ref[...] = (kept_ref[0] * scale).astype(jnp.bfloat16)


def newton_schulz(pieces, rows):
    return pl.pallas_call(
        newton_schulz_kernel,
        out_shape=jax.ShapeDtypeStruct((rows, D), jnp.bfloat16),
        in_specs=[pl.BlockSpec(memory_space=pl.ANY)] * len(pieces),
        out_specs=pl.BlockSpec(memory_space=pltpu.VMEM),
        scratch_shapes=[
            pltpu.VMEM((D, D), jnp.bfloat16),
            pltpu.VMEM((D, D), jnp.bfloat16),
            pltpu.VMEM((D, D), jnp.bfloat16),
            pltpu.VMEM((D, D), jnp.bfloat16),
            pltpu.VMEM((D // TILE, rows, D), jnp.float32),
            pltpu.VMEM((1, TILE // 2), jnp.float32),
            pltpu.VMEM((1, D), jnp.float32),
            pltpu.SemaphoreType.DMA((len(pieces),)),
        ],
        compiler_params=pltpu.CompilerParams(vmem_limit_bytes=40 * 1024 * 1024),
        cost_estimate=pl.CostEstimate(
            flops=2 * ITERS * 7 * D * D * D // 3, bytes_accessed=D * D * 2, transcendentals=0
        ),
        name="newton_schulz",
    )(*pieces)


def body(grad_parts, momentum_owned, owner_table, step_offset):
    replicas, shards = ("y", "x"), ("z", "core")
    mats, piece_rows = grad_parts.shape[1], grad_parts.shape[2]
    sub_rows = momentum_owned.shape[2]
    owner_slot = (owner_table + step_offset[0]) % mats
    slot_ids = jnp.arange(mats, dtype=jnp.int32)
    owner_order = jnp.sum(
        jnp.where(owner_slot[None, :] == slot_ids[:, None], slot_ids[None, :], 0), axis=1
    )
    momentum = momentum_owned[0]

    tall, across = lax.axis_size("y"), lax.axis_size("x")
    parts = grad_parts.reshape(tall, across, piece_rows, D)
    half = piece_rows // 2

    def upper_for(t):
        return lax.dynamic_slice(parts, (0, t, 0, 0), (tall, 1, half, D)).reshape(tall, half, D)

    def lower_for(t):
        return lax.dynamic_slice(parts, (t, 0, half, 0), (1, across, half, D)).reshape(across, half, D)

    (upper, lower), _ = spread_sums([upper_for, lower_for], ["x", "y"])
    (upper, lower), arrived = spread_sums(
        [lambda t: lax.dynamic_index_in_dim(upper, t, 0, False), lambda t: lax.dynamic_index_in_dim(lower, t, 0, False)],
        ["y", "x"],
    )
    summed = lax.optimization_barrier(jnp.concatenate([upper, lower], axis=0))
    grad = summed.astype(jnp.bfloat16)

    by_slot, _ = after(swap(momentum.astype(jnp.bfloat16), shards), arrived)
    own_momentum = swap(pick_blocks(by_slot, owner_slot), replicas).reshape(piece_rows, D)

    grad_float = grad.astype(jnp.float32)
    moment_here = momentum_decay * own_momentum.astype(jnp.float32) + grad_float
    nesterov = (grad_float + momentum_decay * moment_here).astype(jnp.bfloat16)

    pieces = ring_gather(nesterov, "z")

    grad_blocks = swap(grad.reshape(mats, sub_rows, D), replicas)
    grad_blocks, swap_2 = after(grad_blocks, pieces[3])
    ordered, swap_3 = after(pick_blocks(grad_blocks, owner_order), pieces[5])
    grad_rows = swap(ordered, shards)
    swapped = pieces[:3] + [swap_2, pieces[4], swap_3] + pieces[6:]
    both = pieces + [core_swap(piece) for piece in swapped]
    moment = momentum_decay * momentum + grad_rows.astype(jnp.float32)

    update = newton_schulz(both, piece_rows)
    return (update[None], moment[None])


def solution(mesh):
    fine = jax.sharding.Mesh(mesh.devices.reshape(4, 4, 8, 2), ("y", "x", "z", "core"))
    replicas, shards = ("y", "x"), ("z", "core")
    placed = (P(replicas, None, shards, None), P(shards, None, replicas, None), P(), P())
    return jax.shard_map(
        body,
        mesh=fine,
        in_specs=placed,
        out_specs=(P(replicas, shards, None), P(shards, None, replicas, None)),
        check_vma=False,
    )
```

profile of v0, /device:TPU:1, one launch (start us, length us, event | category | flops | bytes accessed | tf_op | source)
XLA Modules:
  0.0 182.5 jit_solution(11605624036061297987)
XLA Ops:
  0.7 1.6 dynamic-slice_bitcast_fusion
  2.2 2.2 %collective-permute-start.6 = (bf16[4,48,1536]{2,1,0:T(8,128)(2,1)S(1)}, bf16[4,48,1536]{2,1,0:T(8,128)(2,1)S(1)}, u32[]{:S(2)}, u32[]{:S(2)}) collective-permute-start(bf16[4,48,1536]{2,1,0:T(8,128)(2,1)S(1)} %get-tuple-element.32), channel_id=1, source_target_pairs={{0,64},{64,128},{128,192},{192,0},{1,65},{65,129},{129,193},{193,1... | collective-permute-start | bytes 1769480 | tf_op jit(solution)/shard_map/ppermute | solution.py:24
  4.4 2.7 %dynamic-slice_bitcast_fusion.5 = (bf16[4,48,1536]{2,1,0:T(8,128)(2,1)}, bf16[4,48,1536]{2,1,0:T(8,128)(2,1)}, bf16[4,48,1536]{2,1,0:T(8,128)(2,1)}) fusion(bf16[4,4,96,1536]{3,2,1,0:T(8,128)(2,1)} %bitcast.62, s32[]{:T(128)S(6)} %select_n.58, s32[]{:T(128)S(6)} %select_n.60, s32[]{:T(128)S(6)} %select_n.59), kind=kLoop, calls=%fused_computation.24 | loop fusion | bytes 3538956 | tf_op jit(solution)/shard_map/reshape | solution.py:216
  9.9 1.5 collective-permute-start.2
  11.4 1.5 collective-permute-start.7
  12.9 4.0 %collective-permute-done.6 = bf16[4,48,1536]{2,1,0:T(8,128)(2,1)S(1)} collective-permute-done((bf16[4,48,1536]{2,1,0:T(8,128)(2,1)S(1)}, bf16[4,48,1536]{2,1,0:T(8,128)(2,1)S(1)}, u32[]{:S(2)}, u32[]{:S(2)}) %collective-permute-start.6) | collective-permute-done | bytes 589856 | tf_op jit(solution)/shard_map/ppermute | solution.py:24
  16.9 3.5 %collective-permute-start.8 = (bf16[4,48,1536]{2,1,0:T(8,128)(2,1)S(1)}, bf16[4,48,1536]{2,1,0:T(8,128)(2,1)}, u32[]{:S(2)}, u32[]{:S(2)}) collective-permute-start(bf16[4,48,1536]{2,1,0:T(8,128)(2,1)S(1)} %get-tuple-element.12), channel_id=1, source_target_pairs={{0,128},{64,192},{128,0},{192,64},{1,129},{65,193},{129,1},{193,65... | collective-permute-start | bytes 1769480 | tf_op jit(solution)/shard_map/ppermute | solution.py:24
  21.4 10.2 %all-to-all-start = ((bf16[16,6,1536]{2,1,0:T(8,128)(2,1)}), bf16[16,6,1536]{2,1,0:T(8,128)(2,1)S(1)}, u32[]{:S(2)}, u32[]{:S(2)}) async-start(bf16[16,6,1536]{2,1,0:T(8,128)(2,1)} %bitcast.59), calls=%async_computation | async-start | bytes 786432 | tf_op jit(solution)/shard_map/all_to_all | solution.py:19
  32.3 3.9 %collective-permute-done.2 = bf16[4,48,1536]{2,1,0:T(8,128)(2,1)} collective-permute-done((bf16[4,48,1536]{2,1,0:T(8,128)(2,1)}, bf16[4,48,1536]{2,1,0:T(8,128)(2,1)}, u32[]{:S(2)}, u32[]{:S(2)}) %collective-permute-start.2) | collective-permute-done | bytes 589856 | tf_op jit(solution)/shard_map/ppermute | solution.py:24
  36.2 2.7 %fusion.3 = (f32[4,48,1536]{2,1,0:T(8,128)S(1)}, f32[4,48,1536]{2,1,0:T(8,128)S(1)}) fusion(bf16[4,48,1536]{2,1,0:T(8,128)(2,1)} %collective-permute-done.2, bf16[4,48,1536]{2,1,0:T(8,128)(2,1)} %collective-permute-done.1, bf16[4,48,1536]{2,1,0:T(8,128)(2,1)} %copy-done.3, bf16[4,4,96,1536]{3,2,1,0:T(8,128)(2,1)} %bitcast.63, s32[]{:T(128)S(6)} %select_n.57, ...), kind=kLoop, calls=%fused_computation.7 | loop fusion | flops 4128768 | bytes 7077896 | tf_op jit(solution)/shard_map/add | solution.py:60
  39.7 2.9 %collective-permute-start.3 = (f32[48,1536]{1,0:T(8,128)}, f32[48,1536]{1,0:T(8,128)}, u32[]{:S(2)}, u32[]{:S(2)}) collective-permute-start(f32[48,1536]{1,0:T(8,128)} %get-tuple-element.34), channel_id=1, source_target_pairs={{0,64},{64,128},{128,192},{192,0},{1,65},{65,129},{129,193},{193,1... | collective-permute-start | bytes 884744 | tf_op jit(solution)/shard_map/ppermute | solution.py:24
  45.7 2.4 %collective-permute-start.10 = (f32[48,1536]{1,0:T(8,128)}, f32[48,1536]{1,0:T(8,128)}, u32[]{:S(2)}, u32[]{:S(2)}) collective-permute-start(f32[48,1536]{1,0:T(8,128)} %get-tuple-element.37), channel_id=1, source_target_pairs={{0,48},{16,0},{32,16},{48,32},{1,49},{17,1},{33,17},{49,33},{2,50}... | collective-permute-start | bytes 884744 | tf_op jit(solution)/shard_map/ppermute | solution.py:24
  48.1 4.4 %collective-permute-done.9 = f32[48,1536]{1,0:T(8,128)S(1)} collective-permute-done((f32[48,1536]{1,0:T(8,128)S(1)}, f32[48,1536]{1,0:T(8,128)S(1)}, u32[]{:S(2)}, u32[]{:S(2)}) %collective-permute-start.9) | collective-permute-done | bytes 294944 | tf_op jit(solution)/shard_map/ppermute | solution.py:24
  54.8 5.9 %all-to-all-start.1 = ((bf16[16,6,1536]{2,1,0:T(8,128)(2,1)}), bf16[16,6,1536]{2,1,0:T(8,128)(2,1)S(1)}, u32[]{:S(2)}, u32[]{:S(2)}) async-start(bf16[16,6,1536]{2,1,0:T(8,128)(2,1)} %gather_fusion), calls=%async_computation.1 | async-start | bytes 786432 | tf_op jit(solution)/shard_map/all_to_all | solution.py:19
  60.7 1.9 %fusion.13 = bf16[48,1536]{1,0:T(8,128)(2,1)} fusion(f32[48,1536]{1,0:T(8,128)} %collective-permute-done.5, f32[48,1536]{1,0:T(8,128)} %collective-permute-done.4, f32[48,1536]{1,0:T(8,128)} %collective-permute-done.3, f32[4,48,1536]{2,1,0:T(8,128)S(1)} %get-tuple-element.26, s32[]{:T(128)S(6)} %select_n.61), kind=kLoop, calls=%fused_computation.31 | loop fusion | flops 294912 | bytes 1327108 | tf_op jit(solution)/shard_map/add | solution.py:60
  62.6 6.6 %all-to-all-done.1 = bf16[16,6,1536]{2,1,0:T(8,128)(2,1)S(1)} async-done(((bf16[16,6,1536]{2,1,0:T(8,128)(2,1)}), bf16[16,6,1536]{2,1,0:T(8,128)(2,1)S(1)}, u32[]{:S(2)}, u32[]{:S(2)}) %all-to-all-start.1) | async-done | bytes 294944 | tf_op jit(solution)/shard_map/all_to_all | solution.py:19
  70.7 1.7 collective-permute-start.12
  72.4 4.2 %collective-permute-start.13 = (bf16[96,1536]{1,0:T(8,128)(2,1)S(1)}, bf16[96,1536]{1,0:T(8,128)(2,1)S(1)}, u32[]{:S(2)}, u32[]{:S(2)}) collective-permute-start(bf16[96,1536]{1,0:T(8,128)(2,1)S(1)} %fusion.8.refs_0_), channel_id=1, source_target_pairs={{0,14},{2,0},{4,2},{6,4},{8,6},{10,8},{12,10},{14,12},{1,15},{3,1}... | collective-permute-start | bytes 884744 | tf_op jit(solution)/shard_map/ppermute | solution.py:24
  76.6 3.8 %collective-permute-done.12.refs_1_ = bf16[96,1536]{1,0:T(8,128)(2,1)S(1)} collective-permute-done((bf16[96,1536]{1,0:T(8,128)(2,1)S(1)}, bf16[96,1536]{1,0:T(8,128)(2,1)S(1)}, u32[]{:S(2)}, u32[]{:S(2)}) %collective-permute-start.12) | collective-permute-done | bytes 294944 | tf_op jit(solution)/shard_map/ppermute | solution.py:24
  80.5 2.9 %collective-permute-start.15 = (bf16[96,1536]{1,0:T(8,128)(2,1)S(1)}, bf16[96,1536]{1,0:T(8,128)(2,1)S(1)}, u32[]{:S(2)}, u32[]{:S(2)}) collective-permute-start(bf16[96,1536]{1,0:T(8,128)(2,1)S(1)} %collective-permute-done.13.refs_2_), channel_id=1, source_target_pairs={{0,14},{2,0},{4,2},{6,4},{8,6},{10,8},{12,10},{14,12},{1,15},{3,1}... | collective-permute-start | bytes 884744 | tf_op jit(solution)/shard_map/ppermute | solution.py:24
  83.4 6.2 %collective-permute-done.14.refs_3_ = bf16[96,1536]{1,0:T(8,128)(2,1)S(1)} collective-permute-done((bf16[96,1536]{1,0:T(8,128)(2,1)S(1)}, bf16[96,1536]{1,0:T(8,128)(2,1)S(1)}, u32[]{:S(2)}, u32[]{:S(2)}) %collective-permute-start.14) | collective-permute-done | bytes 294944 | tf_op jit(solution)/shard_map/ppermute | solution.py:24
  90.4 3.6 %all-to-all-start.2 = ((bf16[16,6,1536]{2,1,0:T(8,128)(2,1)}), bf16[16,6,1536]{2,1,0:T(8,128)(2,1)S(1)}, u32[]{:S(2)}, u32[]{:S(2)}) async-start(bf16[16,6,1536]{2,1,0:T(8,128)(2,1)} %reshape.62), calls=%async_computation.2 | async-start | bytes 786432 | tf_op jit(solution)/shard_map/all_to_all | solution.py:19
  94.1 10.7 %collective-permute-start.20 = (bf16[96,1536]{1,0:T(8,128)(2,1)S(1)}, bf16[96,1536]{1,0:T(8,128)(2,1)S(1)}, u32[]{:S(2)}, u32[]{:S(2)}) collective-permute-start(bf16[96,1536]{1,0:T(8,128)(2,1)S(1)} %fusion.8.refs_0_), channel_id=1, source_target_pairs={{0,1},{1,0},{2,3},{3,2},{4,5},{5,4},{6,7},{7,6},{8,9},{9,8},{10,11... | collective-permute-start | bytes 884744 | tf_op jit(solution)/shard_map/ppermute | solution.py:28
  106.1 8.6 %collective-permute-start.23 = (bf16[96,1536]{1,0:T(8,128)(2,1)S(1)}, bf16[96,1536]{1,0:T(8,128)(2,1)S(1)}, u32[]{:S(2)}, u32[]{:S(2)}) collective-permute-start(bf16[96,1536]{1,0:T(8,128)(2,1)S(1)} %collective-permute-done.14.refs_3_), channel_id=1, source_target_pairs={{0,1},{1,0},{2,3},{3,2},{4,5},{5,4},{6,7},{7,6},{8,9},{9,8},{10,11... | collective-permute-start | bytes 884744 | tf_op jit(solution)/shard_map/ppermute | solution.py:28
  114.7 3.0 %collective-permute-start.17 = (bf16[96,1536]{1,0:T(8,128)(2,1)S(1)}, bf16[96,1536]{1,0:T(8,128)(2,1)S(1)}, u32[]{:S(2)}, u32[]{:S(2)}) collective-permute-start(bf16[96,1536]{1,0:T(8,128)(2,1)S(1)} %collective-permute-done.15.refs_4_), channel_id=1, source_target_pairs={{0,14},{2,0},{4,2},{6,4},{8,6},{10,8},{12,10},{14,12},{1,15},{3,1}... | collective-permute-start | bytes 884744 | tf_op jit(solution)/shard_map/ppermute | solution.py:24
  117.7 2.3 %gather_fusion.1 = bf16[16,6,1536]{2,1,0:T(8,128)(2,1)} fusion(bf16[16,6,1536]{2,1,0:T(8,128)(2,1)} %copy-done.1, s32[1024]{0:T(1024)S(1)} %pad_clamp_fusion), kind=kCustom, calls=%fused_computation.1 | custom fusion | bytes 589888 | tf_op jit(solution)/shard_map/gather | solution.py:32
  120.0 4.0 %collective-permute-done.17.refs_6_ = bf16[96,1536]{1,0:T(8,128)(2,1)S(1)} collective-permute-done((bf16[96,1536]{1,0:T(8,128)(2,1)S(1)}, bf16[96,1536]{1,0:T(8,128)(2,1)S(1)}, u32[]{:S(2)}, u32[]{:S(2)}) %collective-permute-start.17) | collective-permute-done | bytes 294944 | tf_op jit(solution)/shard_map/ppermute | solution.py:24
  125.6 3.4 %collective-permute-start.19 = (bf16[48,1536]{1,0:T(8,128)(2,1)S(1)}, bf16[48,1536]{1,0:T(8,128)(2,1)}, u32[]{:S(2)}, u32[]{:S(2)}) collective-permute-start(bf16[48,1536]{1,0:T(8,128)(2,1)S(1)} %slice.13), channel_id=1, source_target_pairs={{0,14},{2,0},{4,2},{6,4},{8,6},{10,8},{12,10},{14,12},{1,15},{3,1}... | collective-permute-start | bytes 442376 | tf_op jit(solution)/shard_map/ppermute | solution.py:24
  129.1 3.4 %collective-permute-done.18.refs_7_ = bf16[48,1536]{1,0:T(8,128)(2,1)} collective-permute-done((bf16[48,1536]{1,0:T(8,128)(2,1)S(1)}, bf16[48,1536]{1,0:T(8,128)(2,1)}, u32[]{:S(2)}, u32[]{:S(2)}) %collective-permute-start.18) | collective-permute-done | bytes 147488 | tf_op jit(solution)/shard_map/ppermute | solution.py:24
  133.9 6.3 %all-to-all-start.3 = ((bf16[16,6,1536]{2,1,0:T(8,128)(2,1)}), bf16[16,6,1536]{2,1,0:T(8,128)(2,1)}, u32[]{:S(2)}, u32[]{:S(2)}) async-start(bf16[16,6,1536]{2,1,0:T(8,128)(2,1)} %gather_fusion.1), calls=%async_computation.3 | async-start | bytes 786432 | tf_op jit(solution)/shard_map/all_to_all | solution.py:19
  140.3 39.5 %newton_schulz.1 = bf16[96,1536]{1,0:T(8,128)(2,1)} custom-call(bf16[96,1536]{1,0:T(8,128)(2,1)S(1)} %fusion.8.refs_0_, bf16[96,1536]{1,0:T(8,128)(2,1)S(1)} %collective-permute-done.12.refs_1_, bf16[96,1536]{1,0:T(8,128)(2,1)S(1)} %collective-permute-done.13.refs_2_, bf16[96,1536]{1,0:T(8,128)(2,1)S(1)} %collective-permute-done.14.refs_3_, ...), custom_call_target="tpu_custom_call" | custom-call | flops 33822867456 | bytes 4718592 | tf_op jit(solution)/shard_map/newton_schulz/pallas_call | solution.py:177
  179.8 1.6 fusion.6
  (73 shorter events, 17.6 us)
Async XLA Ops:
  2.2 14.7 %collective-permute-start.6 = (bf16[4,48,1536]{2,1,0:T(8,128)(2,1)S(1)}, bf16[4,48,1536]{2,1,0:T(8,128)(2,1)S(1)}, u32[]{:S(2)}, u32[]{:S(2)}) collective-permute-start(bf16[4,48,1536]{2,1,0:T(8,128)(2,1)S(1)} %get-tuple-element.32), channel_id=1, source_target_pairs={{0,64},{64,128},{128,192},{192,0},{1,65},{65,129},{129,193},{193,1... | collective-permute-start | bytes 1769480 | tf_op jit(solution)/shard_map/ppermute | solution.py:24
  7.2 25.1 %collective-permute-start = (bf16[4,48,1536]{2,1,0:T(8,128)(2,1)}, bf16[4,48,1536]{2,1,0:T(8,128)(2,1)S(1)}, u32[]{:S(2)}, u32[]{:S(2)}) collective-permute-start(bf16[4,48,1536]{2,1,0:T(8,128)(2,1)} %get-tuple-element.28), channel_id=1, source_target_pairs={{0,16},{16,32},{32,48},{48,0},{1,17},{17,33},{33,49},{49,1},{2,18}... | collective-permute-start | bytes 1769480 | tf_op jit(solution)/shard_map/ppermute | solution.py:24
  8.4 23.9 %collective-permute-start.1 = (bf16[4,48,1536]{2,1,0:T(8,128)(2,1)}, bf16[4,48,1536]{2,1,0:T(8,128)(2,1)}, u32[]{:S(2)}, u32[]{:S(2)}) collective-permute-start(bf16[4,48,1536]{2,1,0:T(8,128)(2,1)} %get-tuple-element.30), channel_id=1, source_target_pairs={{0,48},{16,0},{32,16},{48,32},{1,49},{17,1},{33,17},{49,33},{2,50}... | collective-permute-start | bytes 1769480 | tf_op jit(solution)/shard_map/ppermute | solution.py:24
  9.9 26.4 %collective-permute-start.2 = (bf16[4,48,1536]{2,1,0:T(8,128)(2,1)}, bf16[4,48,1536]{2,1,0:T(8,128)(2,1)}, u32[]{:S(2)}, u32[]{:S(2)}) collective-permute-start(bf16[4,48,1536]{2,1,0:T(8,128)(2,1)} %get-tuple-element.29), channel_id=1, source_target_pairs={{0,32},{16,48},{32,0},{48,16},{1,33},{17,49},{33,1},{49,17},{2,34}... | collective-permute-start | bytes 1769480 | tf_op jit(solution)/shard_map/ppermute | solution.py:24
  11.4 24.8 %collective-permute-start.7 = (bf16[4,48,1536]{2,1,0:T(8,128)(2,1)S(1)}, bf16[4,48,1536]{2,1,0:T(8,128)(2,1)}, u32[]{:S(2)}, u32[]{:S(2)}) collective-permute-start(bf16[4,48,1536]{2,1,0:T(8,128)(2,1)S(1)} %get-tuple-element.31), channel_id=1, source_target_pairs={{0,192},{64,0},{128,64},{192,128},{1,193},{65,1},{129,65},{193,129... | collective-permute-start | bytes 1769480 | tf_op jit(solution)/shard_map/ppermute | solution.py:24
  16.9 19.3 %collective-permute-start.8 = (bf16[4,48,1536]{2,1,0:T(8,128)(2,1)S(1)}, bf16[4,48,1536]{2,1,0:T(8,128)(2,1)}, u32[]{:S(2)}, u32[]{:S(2)}) collective-permute-start(bf16[4,48,1536]{2,1,0:T(8,128)(2,1)S(1)} %get-tuple-element.12), channel_id=1, source_target_pairs={{0,128},{64,192},{128,0},{192,64},{1,129},{65,193},{129,1},{193,65... | collective-permute-start | bytes 1769480 | tf_op jit(solution)/shard_map/ppermute | solution.py:24
  21.4 32.0 %all-to-all-start = ((bf16[16,6,1536]{2,1,0:T(8,128)(2,1)}), bf16[16,6,1536]{2,1,0:T(8,128)(2,1)S(1)}, u32[]{:S(2)}, u32[]{:S(2)}) async-start(bf16[16,6,1536]{2,1,0:T(8,128)(2,1)} %bitcast.59), calls=%async_computation | async-start | bytes 786432 | tf_op jit(solution)/shard_map/all_to_all | solution.py:19
  39.7 21.0 %collective-permute-start.3 = (f32[48,1536]{1,0:T(8,128)}, f32[48,1536]{1,0:T(8,128)}, u32[]{:S(2)}, u32[]{:S(2)}) collective-permute-start(f32[48,1536]{1,0:T(8,128)} %get-tuple-element.34), channel_id=1, source_target_pairs={{0,64},{64,128},{128,192},{192,0},{1,65},{65,129},{129,193},{193,1... | collective-permute-start | bytes 884744 | tf_op jit(solution)/shard_map/ppermute | solution.py:24
  42.7 18.1 %collective-permute-start.4 = (f32[48,1536]{1,0:T(8,128)S(1)}, f32[48,1536]{1,0:T(8,128)}, u32[]{:S(2)}, u32[]{:S(2)}) collective-permute-start(f32[48,1536]{1,0:T(8,128)S(1)} %get-tuple-element.36), channel_id=1, source_target_pairs={{0,192},{64,0},{128,64},{192,128},{1,193},{65,1},{129,65},{193,129... | collective-permute-start | bytes 884744 | tf_op jit(solution)/shard_map/ppermute | solution.py:24
  43.1 17.6 %collective-permute-start.5 = (f32[48,1536]{1,0:T(8,128)S(1)}, f32[48,1536]{1,0:T(8,128)}, u32[]{:S(2)}, u32[]{:S(2)}) collective-permute-start(f32[48,1536]{1,0:T(8,128)S(1)} %get-tuple-element.35), channel_id=1, source_target_pairs={{0,128},{64,192},{128,0},{192,64},{1,129},{65,193},{129,1},{193,65... | collective-permute-start | bytes 884744 | tf_op jit(solution)/shard_map/ppermute | solution.py:24
  45.3 7.2 %collective-permute-start.9 = (f32[48,1536]{1,0:T(8,128)S(1)}, f32[48,1536]{1,0:T(8,128)S(1)}, u32[]{:S(2)}, u32[]{:S(2)}) collective-permute-start(f32[48,1536]{1,0:T(8,128)S(1)} %get-tuple-element.38), channel_id=1, source_target_pairs={{0,16},{16,32},{32,48},{48,0},{1,17},{17,33},{33,49},{49,1},{2,18}... | collective-permute-start | bytes 884744 | tf_op jit(solution)/shard_map/ppermute | solution.py:24
  45.7 23.7 %collective-permute-start.10 = (f32[48,1536]{1,0:T(8,128)}, f32[48,1536]{1,0:T(8,128)}, u32[]{:S(2)}, u32[]{:S(2)}) collective-permute-start(f32[48,1536]{1,0:T(8,128)} %get-tuple-element.37), channel_id=1, source_target_pairs={{0,48},{16,0},{32,16},{48,32},{1,49},{17,1},{33,17},{49,33},{2,50}... | collective-permute-start | bytes 884744 | tf_op jit(solution)/shard_map/ppermute | solution.py:24
  53.2 16.2 %collective-permute-start.11 = (f32[48,1536]{1,0:T(8,128)}, f32[48,1536]{1,0:T(8,128)}, u32[]{:S(2)}, u32[]{:S(2)}) collective-permute-start(f32[48,1536]{1,0:T(8,128)} %get-tuple-element.14), channel_id=1, source_target_pairs={{0,32},{16,48},{32,0},{48,16},{1,33},{17,49},{33,1},{49,17},{2,34}... | collective-permute-start | bytes 884744 | tf_op jit(solution)/shard_map/ppermute | solution.py:24
  54.8 14.4 %all-to-all-start.1 = ((bf16[16,6,1536]{2,1,0:T(8,128)(2,1)}), bf16[16,6,1536]{2,1,0:T(8,128)(2,1)S(1)}, u32[]{:S(2)}, u32[]{:S(2)}) async-start(bf16[16,6,1536]{2,1,0:T(8,128)(2,1)} %gather_fusion), calls=%async_computation.1 | async-start | bytes 786432 | tf_op jit(solution)/shard_map/all_to_all | solution.py:19
  70.7 9.8 %collective-permute-start.12 = (bf16[96,1536]{1,0:T(8,128)(2,1)S(1)}, bf16[96,1536]{1,0:T(8,128)(2,1)S(1)}, u32[]{:S(2)}, u32[]{:S(2)}) collective-permute-start(bf16[96,1536]{1,0:T(8,128)(2,1)S(1)} %fusion.8.refs_0_), channel_id=1, source_target_pairs={{0,2},{2,4},{4,6},{6,8},{8,10},{10,12},{12,14},{14,0},{1,3},{3,5},... | collective-permute-start | bytes 884744 | tf_op jit(solution)/shard_map/ppermute | solution.py:24
  72.4 8.1 %collective-permute-start.13 = (bf16[96,1536]{1,0:T(8,128)(2,1)S(1)}, bf16[96,1536]{1,0:T(8,128)(2,1)S(1)}, u32[]{:S(2)}, u32[]{:S(2)}) collective-permute-start(bf16[96,1536]{1,0:T(8,128)(2,1)S(1)} %fusion.8.refs_0_), channel_id=1, source_target_pairs={{0,14},{2,0},{4,2},{6,4},{8,6},{10,8},{12,10},{14,12},{1,15},{3,1}... | collective-permute-start | bytes 884744 | tf_op jit(solution)/shard_map/ppermute | solution.py:24
  80.5 9.1 %collective-permute-start.14 = (bf16[96,1536]{1,0:T(8,128)(2,1)S(1)}, bf16[96,1536]{1,0:T(8,128)(2,1)S(1)}, u32[]{:S(2)}, u32[]{:S(2)}) collective-permute-start(bf16[96,1536]{1,0:T(8,128)(2,1)S(1)} %collective-permute-done.12.refs_1_), channel_id=1, source_target_pairs={{0,2},{2,4},{4,6},{6,8},{8,10},{10,12},{12,14},{14,0},{1,3},{3,5},... | collective-permute-start | bytes 884744 | tf_op jit(solution)/shard_map/ppermute | solution.py:24
  80.5 25.6 %collective-permute-start.15 = (bf16[96,1536]{1,0:T(8,128)(2,1)S(1)}, bf16[96,1536]{1,0:T(8,128)(2,1)S(1)}, u32[]{:S(2)}, u32[]{:S(2)}) collective-permute-start(bf16[96,1536]{1,0:T(8,128)(2,1)S(1)} %collective-permute-done.13.refs_2_), channel_id=1, source_target_pairs={{0,14},{2,0},{4,2},{6,4},{8,6},{10,8},{12,10},{14,12},{1,15},{3,1}... | collective-permute-start | bytes 884744 | tf_op jit(solution)/shard_map/ppermute | solution.py:24
  89.6 25.2 %collective-permute-start.16 = (bf16[96,1536]{1,0:T(8,128)(2,1)S(1)}, bf16[96,1536]{1,0:T(8,128)(2,1)S(1)}, u32[]{:S(2)}, u32[]{:S(2)}) collective-permute-start(bf16[96,1536]{1,0:T(8,128)(2,1)S(1)} %collective-permute-done.14.refs_3_), channel_id=1, source_target_pairs={{0,2},{2,4},{4,6},{6,8},{8,10},{10,12},{12,14},{14,0},{1,3},{3,5},... | collective-permute-start | bytes 884744 | tf_op jit(solution)/shard_map/ppermute | solution.py:24
  90.4 14.9 %all-to-all-start.2 = ((bf16[16,6,1536]{2,1,0:T(8,128)(2,1)}), bf16[16,6,1536]{2,1,0:T(8,128)(2,1)S(1)}, u32[]{:S(2)}, u32[]{:S(2)}) async-start(bf16[16,6,1536]{2,1,0:T(8,128)(2,1)} %reshape.62), calls=%async_computation.2 | async-start | bytes 786432 | tf_op jit(solution)/shard_map/all_to_all | solution.py:19
  94.1 30.8 %collective-permute-start.20 = (bf16[96,1536]{1,0:T(8,128)(2,1)S(1)}, bf16[96,1536]{1,0:T(8,128)(2,1)S(1)}, u32[]{:S(2)}, u32[]{:S(2)}) collective-permute-start(bf16[96,1536]{1,0:T(8,128)(2,1)S(1)} %fusion.8.refs_0_), channel_id=1, source_target_pairs={{0,1},{1,0},{2,3},{3,2},{4,5},{5,4},{6,7},{7,6},{8,9},{9,8},{10,11... | collective-permute-start | bytes 884744 | tf_op jit(solution)/shard_map/ppermute | solution.py:28
  104.8 20.2 %collective-permute-start.21 = (bf16[96,1536]{1,0:T(8,128)(2,1)S(1)}, bf16[96,1536]{1,0:T(8,128)(2,1)S(1)}, u32[]{:S(2)}, u32[]{:S(2)}) collective-permute-start(bf16[96,1536]{1,0:T(8,128)(2,1)S(1)} %collective-permute-done.12.refs_1_), channel_id=1, source_target_pairs={{0,1},{1,0},{2,3},{3,2},{4,5},{5,4},{6,7},{7,6},{8,9},{9,8},{10,11... | collective-permute-start | bytes 884744 | tf_op jit(solution)/shard_map/ppermute | solution.py:28
  104.9 20.2 %collective-permute-start.22 = (bf16[96,1536]{1,0:T(8,128)(2,1)S(1)}, bf16[96,1536]{1,0:T(8,128)(2,1)S(1)}, u32[]{:S(2)}, u32[]{:S(2)}) collective-permute-start(bf16[96,1536]{1,0:T(8,128)(2,1)S(1)} %collective-permute-done.13.refs_2_), channel_id=1, source_target_pairs={{0,1},{1,0},{2,3},{3,2},{4,5},{5,4},{6,7},{7,6},{8,9},{9,8},{10,11... | collective-permute-start | bytes 884744 | tf_op jit(solution)/shard_map/ppermute | solution.py:28
  106.1 19.6 %collective-permute-start.23 = (bf16[96,1536]{1,0:T(8,128)(2,1)S(1)}, bf16[96,1536]{1,0:T(8,128)(2,1)S(1)}, u32[]{:S(2)}, u32[]{:S(2)}) collective-permute-start(bf16[96,1536]{1,0:T(8,128)(2,1)S(1)} %collective-permute-done.14.refs_3_), channel_id=1, source_target_pairs={{0,1},{1,0},{2,3},{3,2},{4,5},{5,4},{6,7},{7,6},{8,9},{9,8},{10,11... | collective-permute-start | bytes 884744 | tf_op jit(solution)/shard_map/ppermute | solution.py:28
  114.7 9.3 %collective-permute-start.17 = (bf16[96,1536]{1,0:T(8,128)(2,1)S(1)}, bf16[96,1536]{1,0:T(8,128)(2,1)S(1)}, u32[]{:S(2)}, u32[]{:S(2)}) collective-permute-start(bf16[96,1536]{1,0:T(8,128)(2,1)S(1)} %collective-permute-done.15.refs_4_), channel_id=1, source_target_pairs={{0,14},{2,0},{4,2},{6,4},{8,6},{10,8},{12,10},{14,12},{1,15},{3,1}... | collective-permute-start | bytes 884744 | tf_op jit(solution)/shard_map/ppermute | solution.py:24
  124.1 16.2 %collective-permute-start.24 = (bf16[96,1536]{1,0:T(8,128)(2,1)S(1)}, bf16[96,1536]{1,0:T(8,128)(2,1)S(1)}, u32[]{:S(2)}, u32[]{:S(2)}) collective-permute-start(bf16[96,1536]{1,0:T(8,128)(2,1)S(1)} %collective-permute-done.15.refs_4_), channel_id=1, source_target_pairs={{0,1},{1,0},{2,3},{3,2},{4,5},{5,4},{6,7},{7,6},{8,9},{9,8},{10,11... | collective-permute-start | bytes 884744 | tf_op jit(solution)/shard_map/ppermute | solution.py:28
  124.9 15.3 %collective-permute-start.25 = (bf16[96,1536]{1,0:T(8,128)(2,1)S(1)}, bf16[96,1536]{1,0:T(8,128)(2,1)}, u32[]{:S(2)}, u32[]{:S(2)}) collective-permute-start(bf16[96,1536]{1,0:T(8,128)(2,1)S(1)} %collective-permute-done.16.refs_5_), channel_id=1, source_target_pairs={{0,1},{1,0},{2,3},{3,2},{4,5},{5,4},{6,7},{7,6},{8,9},{9,8},{10,11... | collective-permute-start | bytes 884744 | tf_op jit(solution)/shard_map/ppermute | solution.py:28
  125.1 7.5 %collective-permute-start.18 = (bf16[48,1536]{1,0:T(8,128)(2,1)S(1)}, bf16[48,1536]{1,0:T(8,128)(2,1)}, u32[]{:S(2)}, u32[]{:S(2)}) collective-permute-start(bf16[48,1536]{1,0:T(8,128)(2,1)S(1)} %slice.12), channel_id=1, source_target_pairs={{0,2},{2,4},{4,6},{6,8},{8,10},{10,12},{12,14},{14,0},{1,3},{3,5},... | collective-permute-start | bytes 442376 | tf_op jit(solution)/shard_map/ppermute | solution.py:24
  125.2 15.1 %collective-permute-start.26 = (bf16[96,1536]{1,0:T(8,128)(2,1)S(1)}, bf16[96,1536]{1,0:T(8,128)(2,1)}, u32[]{:S(2)}, u32[]{:S(2)}) collective-permute-start(bf16[96,1536]{1,0:T(8,128)(2,1)S(1)} %collective-permute-done.17.refs_6_), channel_id=1, source_target_pairs={{0,1},{1,0},{2,3},{3,2},{4,5},{5,4},{6,7},{7,6},{8,9},{9,8},{10,11... | collective-permute-start | bytes 884744 | tf_op jit(solution)/shard_map/ppermute | solution.py:28
  125.6 7.8 %collective-permute-start.19 = (bf16[48,1536]{1,0:T(8,128)(2,1)S(1)}, bf16[48,1536]{1,0:T(8,128)(2,1)}, u32[]{:S(2)}, u32[]{:S(2)}) collective-permute-start(bf16[48,1536]{1,0:T(8,128)(2,1)S(1)} %slice.13), channel_id=1, source_target_pairs={{0,14},{2,0},{4,2},{6,4},{8,6},{10,8},{12,10},{14,12},{1,15},{3,1}... | collective-permute-start | bytes 442376 | tf_op jit(solution)/shard_map/ppermute | solution.py:24
  132.5 7.7 %collective-permute-start.27 = (bf16[48,1536]{1,0:T(8,128)(2,1)}, bf16[48,1536]{1,0:T(8,128)(2,1)}, u32[]{:S(2)}, u32[]{:S(2)}) collective-permute-start(bf16[48,1536]{1,0:T(8,128)(2,1)} %collective-permute-done.18.refs_7_), channel_id=1, source_target_pairs={{0,1},{1,0},{2,3},{3,2},{4,5},{5,4},{6,7},{7,6},{8,9},{9,8},{10,11... | collective-permute-start | bytes 442376 | tf_op jit(solution)/shard_map/ppermute | solution.py:28
  133.9 45.8 %all-to-all-start.3 = ((bf16[16,6,1536]{2,1,0:T(8,128)(2,1)}), bf16[16,6,1536]{2,1,0:T(8,128)(2,1)}, u32[]{:S(2)}, u32[]{:S(2)}) async-start(bf16[16,6,1536]{2,1,0:T(8,128)(2,1)} %gather_fusion.1), calls=%async_computation.3 | async-start | bytes 786432 | tf_op jit(solution)/shard_map/all_to_all | solution.py:19
  (8 other events, 42.2 us)
where the time goes:
time: 183 us
  starting transfers between devices  83.1 us (45%)
  Pallas kernels  39.5 us (22%)
  waiting for transfers between devices  36.5 us (20%)
  local copies, waits for them, and re-layouts  14.3 us (8%)
  other arithmetic  7.61 us (4%)
    pallas_call x1, Pallas kernels, newton_schulz(): pl.pallas_call(newton_schulz_kernel, out_shape=jax.ShapeDtypeStruct((rows...  39.5 us
    ppermute x20, starting transfers between devices, shift(): lax.ppermute(value, axis, [(i, (i + by) % count) for i in range(count)])  34.4 us
    ppermute x20, waiting for transfers between devices, shift(): lax.ppermute(value, axis, [(i, (i + by) % count) for i in range(count)])  29.8 us
    all_to_all x4, starting transfers between devices, swap(): return lax.all_to_all(value, axis, split_axis=0, concat_axis=0, tiled=True)  26 us
    ppermute x9, starting transfers between devices, core_swap(): return lax.ppermute(value, 'core', [(0, 1), (1, 0)])  22.7 us
    all_to_all x4, waiting for transfers between devices, swap(): return lax.all_to_all(value, axis, split_axis=0, concat_axis=0, tiled=True)  6.61 us
    add x3, other arithmetic, spread_sums(): total = total + part.astype(jnp.float32)  5.66 us
    unnamed x16, local copies, waits for them, and re-layouts  3.72 us
  transfers between devices with their start and end apart: 33, of which 8 were waited for; matrix products, arithmetic and copies ran while one was open for 8% of the time, Pallas kernels for 22%

commit v1 on v0

--- a/solution.py
+++ b/solution.py
@@ -234,13 +234,11 @@
     nesterov = (grad_float + momentum_decay * moment_here).astype(jnp.bfloat16)
 
     pieces = ring_gather(nesterov, "z")
+    both = pieces + [core_swap(piece) for piece in pieces]
 
     grad_blocks = swap(grad.reshape(mats, sub_rows, D), replicas)
-    grad_blocks, swap_2 = after(grad_blocks, pieces[3])
-    ordered, swap_3 = after(pick_blocks(grad_blocks, owner_order), pieces[5])
-    grad_rows = swap(ordered, shards)
-    swapped = pieces[:3] + [swap_2, pieces[4], swap_3] + pieces[6:]
-    both = pieces + [core_swap(piece) for piece in swapped]
+    grad_blocks, _ = after(grad_blocks, pieces[-3])
+    grad_rows = swap(jnp.take(grad_blocks, owner_order, axis=0), shards)
     moment = momentum_decay * momentum + grad_rows.astype(jnp.float32)
 
     update = newton_schulz(both, piece_rows)

time: 183 us -> 169 us (0.923)
  waiting for transfers between devices: 36.5 us -> 23.1 us
  starting transfers between devices: 83.1 us -> 80.9 us
    ppermute x20, waiting for transfers between devices: 29.8 us -> 16 us  [shift(): lax.ppermute(value, axis, [(i, (i + by) % count) for i in range(count)])]
    gather x0 -> x1, local copies, waits for them, and re-layouts: none -> 2.31 us  [body(): grad_rows = swap(jnp.take(grad_blocks, owner_order, axis=0), shards)]
    gather x2 -> x1, local copies, waits for them, and re-layouts: 3.63 us -> 1.32 us  [pick_blocks(): return blocks.at[order].get(mode='promise_in_bounds')]
    select_n x0 -> x2, other arithmetic: none -> 1.86 us  [body(): grad_rows = swap(jnp.take(grad_blocks, owner_order, axis=0), shards)]
    unnamed x16 -> x10, local copies, waits for them, and re-layouts: 3.72 us -> 2.97 us
  transfers between devices with their start and end apart: 33 -> 33, of which waited for: 8 -> 5; matrix products, arithmetic and copies ran while one was open for 8% -> 10% of each run, Pallas kernels for 22% -> 23%
where the time goes in v1:
time: 169 us
  starting transfers between devices  80.9 us (48%)
  Pallas kernels  39.5 us (23%)
  waiting for transfers between devices  23.1 us (14%)
  local copies, waits for them, and re-layouts  14.9 us (9%)
  other arithmetic  8.9 us (5%)
    pallas_call x1, Pallas kernels, newton_schulz(): pl.pallas_call(newton_schulz_kernel, out_shape=jax.ShapeDtypeStruct((rows...  39.5 us
    ppermute x20, starting transfers between devices, shift(): lax.ppermute(value, axis, [(i, (i + by) % count) for i in range(count)])  33.5 us
    all_to_all x4, starting transfers between devices, swap(): return lax.all_to_all(value, axis, split_axis=0, concat_axis=0, tiled=True)  25 us
    ppermute x9, starting transfers between devices, core_swap(): return lax.ppermute(value, 'core', [(0, 1), (1, 0)])  22.4 us
    ppermute x20, waiting for transfers between devices, shift(): lax.ppermute(value, axis, [(i, (i + by) % count) for i in range(count)])  16 us
    all_to_all x4, waiting for transfers between devices, swap(): return lax.all_to_all(value, axis, split_axis=0, concat_axis=0, tiled=True)  7.04 us
    add x3, other arithmetic, spread_sums(): total = total + part.astype(jnp.float32)  5.1 us
  transfers between devices with their start and end apart: 33, of which 5 were waited for; matrix products, arithmetic and copies ran while one was open for 10% of the time, Pallas kernels for 23%

profile of v1, /device:TPU:1, one launch (start us, length us, event | category | flops | bytes accessed | tf_op | source)
XLA Modules:
  0.0 168.7 jit_solution(15080053396459635929)
XLA Ops:
  0.7 1.6 dynamic-slice_bitcast_fusion
  2.2 2.2 %collective-permute-start.6 = (bf16[4,48,1536]{2,1,0:T(8,128)(2,1)S(1)}, bf16[4,48,1536]{2,1,0:T(8,128)(2,1)S(1)}, u32[]{:S(2)}, u32[]{:S(2)}) collective-permute-start(bf16[4,48,1536]{2,1,0:T(8,128)(2,1)S(1)} %get-tuple-element.26), channel_id=1, source_target_pairs={{0,64},{64,128},{128,192},{192,0},{1,65},{65,129},{129,193},{193,1... | collective-permute-start | bytes 1769480 | tf_op jit(solution)/shard_map/ppermute | solution.py:24
  4.4 2.8 %dynamic-slice_bitcast_fusion.5 = (bf16[4,48,1536]{2,1,0:T(8,128)(2,1)}, bf16[4,48,1536]{2,1,0:T(8,128)(2,1)}, bf16[4,48,1536]{2,1,0:T(8,128)(2,1)}) fusion(bf16[4,4,96,1536]{3,2,1,0:T(8,128)(2,1)} %bitcast.62, s32[]{:T(128)S(6)} %select_n.68, s32[]{:T(128)S(6)} %select_n.70, s32[]{:T(128)S(6)} %select_n.69), kind=kLoop, calls=%fused_computation.24 | loop fusion | bytes 3538956 | tf_op jit(solution)/shard_map/reshape | solution.py:216
  8.4 1.5 collective-permute-start.1
  9.9 1.5 collective-permute-start.2
  11.4 1.5 collective-permute-start.7
  12.9 4.0 %collective-permute-done.6 = bf16[4,48,1536]{2,1,0:T(8,128)(2,1)S(1)} collective-permute-done((bf16[4,48,1536]{2,1,0:T(8,128)(2,1)S(1)}, bf16[4,48,1536]{2,1,0:T(8,128)(2,1)S(1)}, u32[]{:S(2)}, u32[]{:S(2)}) %collective-permute-start.6) | collective-permute-done | bytes 589856 | tf_op jit(solution)/shard_map/ppermute | solution.py:24
  16.9 3.5 %collective-permute-start.8 = (bf16[4,48,1536]{2,1,0:T(8,128)(2,1)S(1)}, bf16[4,48,1536]{2,1,0:T(8,128)(2,1)}, u32[]{:S(2)}, u32[]{:S(2)}) collective-permute-start(bf16[4,48,1536]{2,1,0:T(8,128)(2,1)S(1)} %get-tuple-element.9), channel_id=1, source_target_pairs={{0,128},{64,192},{128,0},{192,64},{1,129},{65,193},{129,1},{193,65... | collective-permute-start | bytes 1769480 | tf_op jit(solution)/shard_map/ppermute | solution.py:24
  21.4 10.2 %all-to-all-start = ((bf16[16,6,1536]{2,1,0:T(8,128)(2,1)}), bf16[16,6,1536]{2,1,0:T(8,128)(2,1)S(1)}, u32[]{:S(2)}, u32[]{:S(2)}) async-start(bf16[16,6,1536]{2,1,0:T(8,128)(2,1)} %bitcast.59), calls=%async_computation | async-start | bytes 786432 | tf_op jit(solution)/shard_map/all_to_all | solution.py:19
  32.3 3.9 %collective-permute-done.2 = bf16[4,48,1536]{2,1,0:T(8,128)(2,1)} collective-permute-done((bf16[4,48,1536]{2,1,0:T(8,128)(2,1)}, bf16[4,48,1536]{2,1,0:T(8,128)(2,1)}, u32[]{:S(2)}, u32[]{:S(2)}) %collective-permute-start.2) | collective-permute-done | bytes 589856 | tf_op jit(solution)/shard_map/ppermute | solution.py:24
  36.2 2.7 %fusion.3 = (f32[4,48,1536]{2,1,0:T(8,128)S(1)}, f32[4,48,1536]{2,1,0:T(8,128)S(1)}) fusion(bf16[4,48,1536]{2,1,0:T(8,128)(2,1)} %collective-permute-done.2, bf16[4,48,1536]{2,1,0:T(8,128)(2,1)} %collective-permute-done.1, bf16[4,48,1536]{2,1,0:T(8,128)(2,1)} %copy-done.1, bf16[4,4,96,1536]{3,2,1,0:T(8,128)(2,1)} %bitcast.63, s32[]{:T(128)S(6)} %select_n.67, ...), kind=kLoop, calls=%fused_computation.7 | loop fusion | flops 4128768 | bytes 7077896 | tf_op jit(solution)/shard_map/add | solution.py:60
  39.8 2.9 %collective-permute-start.3 = (f32[48,1536]{1,0:T(8,128)}, f32[48,1536]{1,0:T(8,128)}, u32[]{:S(2)}, u32[]{:S(2)}) collective-permute-start(f32[48,1536]{1,0:T(8,128)} %get-tuple-element.28), channel_id=1, source_target_pairs={{0,64},{64,128},{128,192},{192,0},{1,65},{65,129},{129,193},{193,1... | collective-permute-start | bytes 884744 | tf_op jit(solution)/shard_map/ppermute | solution.py:24
  43.2 1.4 collective-permute-start.5
  45.7 2.4 %collective-permute-start.10 = (f32[48,1536]{1,0:T(8,128)}, f32[48,1536]{1,0:T(8,128)}, u32[]{:S(2)}, u32[]{:S(2)}) collective-permute-start(f32[48,1536]{1,0:T(8,128)} %get-tuple-element.31), channel_id=1, source_target_pairs={{0,48},{16,0},{32,16},{48,32},{1,49},{17,1},{33,17},{49,33},{2,50}... | collective-permute-start | bytes 884744 | tf_op jit(solution)/shard_map/ppermute | solution.py:24
  48.1 4.4 %collective-permute-done.9 = f32[48,1536]{1,0:T(8,128)S(1)} collective-permute-done((f32[48,1536]{1,0:T(8,128)S(1)}, f32[48,1536]{1,0:T(8,128)S(1)}, u32[]{:S(2)}, u32[]{:S(2)}) %collective-permute-start.9) | collective-permute-done | bytes 294944 | tf_op jit(solution)/shard_map/ppermute | solution.py:24
  54.8 5.9 %all-to-all-start.1 = ((bf16[16,6,1536]{2,1,0:T(8,128)(2,1)}), bf16[16,6,1536]{2,1,0:T(8,128)(2,1)S(1)}, u32[]{:S(2)}, u32[]{:S(2)}) async-start(bf16[16,6,1536]{2,1,0:T(8,128)(2,1)} %gather_fusion), calls=%async_computation.1 | async-start | bytes 786432 | tf_op jit(solution)/shard_map/all_to_all | solution.py:19
  62.0 7.0 %all-to-all-done.1 = bf16[16,6,1536]{2,1,0:T(8,128)(2,1)S(1)} async-done(((bf16[16,6,1536]{2,1,0:T(8,128)(2,1)}), bf16[16,6,1536]{2,1,0:T(8,128)(2,1)S(1)}, u32[]{:S(2)}, u32[]{:S(2)}) %all-to-all-start.1) | async-done | bytes 294944 | tf_op jit(solution)/shard_map/all_to_all | solution.py:19
  70.6 5.7 %collective-permute-start.13 = (bf16[96,1536]{1,0:T(8,128)(2,1)S(1)}, bf16[96,1536]{1,0:T(8,128)(2,1)S(1)}, u32[]{:S(2)}, u32[]{:S(2)}) collective-permute-start(bf16[96,1536]{1,0:T(8,128)(2,1)S(1)} %fusion.8.refs_0_), channel_id=1, source_target_pairs={{0,14},{2,0},{4,2},{6,4},{8,6},{10,8},{12,10},{14,12},{1,15},{3,1}... | collective-permute-start | bytes 884744 | tf_op jit(solution)/shard_map/ppermute | solution.py:24
  76.2 3.7 %collective-permute-done.13.refs_2_ = bf16[96,1536]{1,0:T(8,128)(2,1)S(1)} collective-permute-done((bf16[96,1536]{1,0:T(8,128)(2,1)S(1)}, bf16[96,1536]{1,0:T(8,128)(2,1)S(1)}, u32[]{:S(2)}, u32[]{:S(2)}) %collective-permute-start.13) | collective-permute-done | bytes 294944 | tf_op jit(solution)/shard_map/ppermute | solution.py:24
  79.9 3.1 %collective-permute-start.15 = (bf16[96,1536]{1,0:T(8,128)(2,1)S(1)}, bf16[96,1536]{1,0:T(8,128)(2,1)S(1)}, u32[]{:S(2)}, u32[]{:S(2)}) collective-permute-start(bf16[96,1536]{1,0:T(8,128)(2,1)S(1)} %collective-permute-done.13.refs_2_), channel_id=1, source_target_pairs={{0,14},{2,0},{4,2},{6,4},{8,6},{10,8},{12,10},{14,12},{1,15},{3,1}... | collective-permute-start | bytes 884744 | tf_op jit(solution)/shard_map/ppermute | solution.py:24
  83.0 10.5 %collective-permute-start.20 = (bf16[96,1536]{1,0:T(8,128)(2,1)S(1)}, bf16[96,1536]{1,0:T(8,128)(2,1)S(1)}, u32[]{:S(2)}, u32[]{:S(2)}) collective-permute-start(bf16[96,1536]{1,0:T(8,128)(2,1)S(1)} %fusion.8.refs_0_), channel_id=1, source_target_pairs={{0,1},{1,0},{2,3},{3,2},{4,5},{5,4},{6,7},{7,6},{8,9},{9,8},{10,11... | collective-permute-start | bytes 884744 | tf_op jit(solution)/shard_map/ppermute | solution.py:28
  93.5 3.0 %collective-permute-start.17 = (bf16[96,1536]{1,0:T(8,128)(2,1)S(1)}, bf16[96,1536]{1,0:T(8,128)(2,1)S(1)}, u32[]{:S(2)}, u32[]{:S(2)}) collective-permute-start(bf16[96,1536]{1,0:T(8,128)(2,1)S(1)} %collective-permute-done.15.refs_4_), channel_id=1, source_target_pairs={{0,14},{2,0},{4,2},{6,4},{8,6},{10,8},{12,10},{14,12},{1,15},{3,1}... | collective-permute-start | bytes 884744 | tf_op jit(solution)/shard_map/ppermute | solution.py:24
  97.5 4.2 %all-to-all-start.2 = ((bf16[16,6,1536]{2,1,0:T(8,128)(2,1)}), bf16[16,6,1536]{2,1,0:T(8,128)(2,1)}, u32[]{:S(2)}, u32[]{:S(2)}) async-start(bf16[16,6,1536]{2,1,0:T(8,128)(2,1)} %reshape.67), calls=%async_computation.2 | async-start | bytes 786432 | tf_op jit(solution)/shard_map/all_to_all | solution.py:19
  101.7 5.6 %collective-permute-start.21 = (bf16[96,1536]{1,0:T(8,128)(2,1)S(1)}, bf16[96,1536]{1,0:T(8,128)(2,1)S(1)}, u32[]{:S(2)}, u32[]{:S(2)}) collective-permute-start(bf16[96,1536]{1,0:T(8,128)(2,1)S(1)} %collective-permute-done.12.refs_1_), channel_id=1, source_target_pairs={{0,1},{1,0},{2,3},{3,2},{4,5},{5,4},{6,7},{7,6},{8,9},{9,8},{10,11... | collective-permute-start | bytes 884744 | tf_op jit(solution)/shard_map/ppermute | solution.py:28
  107.4 2.6 %collective-permute-start.23 = (bf16[96,1536]{1,0:T(8,128)(2,1)S(1)}, bf16[96,1536]{1,0:T(8,128)(2,1)S(1)}, u32[]{:S(2)}, u32[]{:S(2)}) collective-permute-start(bf16[96,1536]{1,0:T(8,128)(2,1)S(1)} %collective-permute-done.14.refs_3_), channel_id=1, source_target_pairs={{0,1},{1,0},{2,3},{3,2},{4,5},{5,4},{6,7},{7,6},{8,9},{9,8},{10,11... | collective-permute-start | bytes 884744 | tf_op jit(solution)/shard_map/ppermute | solution.py:28
  111.3 2.7 %collective-permute-start.19 = (bf16[48,1536]{1,0:T(8,128)(2,1)}, bf16[48,1536]{1,0:T(8,128)(2,1)}, u32[]{:S(2)}, u32[]{:S(2)}) collective-permute-start(bf16[48,1536]{1,0:T(8,128)(2,1)} %slice.13), channel_id=1, source_target_pairs={{0,14},{2,0},{4,2},{6,4},{8,6},{10,8},{12,10},{14,12},{1,15},{3,1}... | collective-permute-start | bytes 442376 | tf_op jit(solution)/shard_map/ppermute | solution.py:24
  114.0 2.3 %gather_fusion.1 = bf16[16,6,1536]{2,1,0:T(8,128)(2,1)} fusion(bf16[16,6,1536]{2,1,0:T(8,128)(2,1)} %all-to-all-done.2, s32[1024]{0:T(1024)S(1)} %pad_clamp_fusion), kind=kCustom, calls=%fused_computation.1 | custom fusion | bytes 589888 | tf_op jit(solution)/shard_map/jit(_take)/gather | solution.py:241
  116.3 2.6 %collective-permute-start.24 = (bf16[96,1536]{1,0:T(8,128)(2,1)S(1)}, bf16[96,1536]{1,0:T(8,128)(2,1)S(1)}, u32[]{:S(2)}, u32[]{:S(2)}) collective-permute-start(bf16[96,1536]{1,0:T(8,128)(2,1)S(1)} %collective-permute-done.15.refs_4_), channel_id=1, source_target_pairs={{0,1},{1,0},{2,3},{3,2},{4,5},{5,4},{6,7},{7,6},{8,9},{9,8},{10,11... | collective-permute-start | bytes 884744 | tf_op jit(solution)/shard_map/ppermute | solution.py:28
  120.0 1.9 %broadcast_select_fusion = bf16[16,6,1536]{2,1,0:T(8,128)(2,1)} fusion(bf16[16,6,1536]{2,1,0:T(8,128)(2,1)} %gather_fusion.1, pred[16]{0:T(512)(128)(4,1)S(1)} %compare_and_fusion), kind=kLoop, calls=%fused_computation.26 | loop fusion | flops 147456 | bytes 589840 | tf_op jit(solution)/shard_map/jit(_take)/select_n | solution.py:241
  121.8 4.7 %all-to-all-start.3 = ((bf16[16,6,1536]{2,1,0:T(8,128)(2,1)}), bf16[16,6,1536]{2,1,0:T(8,128)(2,1)}, u32[]{:S(2)}, u32[]{:S(2)}) async-start(bf16[16,6,1536]{2,1,0:T(8,128)(2,1)} %broadcast_select_fusion), calls=%async_computation.3 | async-start | bytes 786432 | tf_op jit(solution)/shard_map/all_to_all | solution.py:19
  126.5 39.5 %newton_schulz.1 = bf16[96,1536]{1,0:T(8,128)(2,1)} custom-call(bf16[96,1536]{1,0:T(8,128)(2,1)S(1)} %fusion.8.refs_0_, bf16[96,1536]{1,0:T(8,128)(2,1)S(1)} %collective-permute-done.12.refs_1_, bf16[96,1536]{1,0:T(8,128)(2,1)S(1)} %collective-permute-done.13.refs_2_, bf16[96,1536]{1,0:T(8,128)(2,1)S(1)} %collective-permute-done.14.refs_3_, ...), custom_call_target="tpu_custom_call" | custom-call | flops 33822867456 | bytes 4718592 | tf_op jit(solution)/shard_map/newton_schulz/pallas_call | solution.py:177
  166.0 1.6 fusion.6
  (69 shorter events, 14.4 us)
Async XLA Ops:
  2.2 14.7 %collective-permute-start.6 = (bf16[4,48,1536]{2,1,0:T(8,128)(2,1)S(1)}, bf16[4,48,1536]{2,1,0:T(8,128)(2,1)S(1)}, u32[]{:S(2)}, u32[]{:S(2)}) collective-permute-start(bf16[4,48,1536]{2,1,0:T(8,128)(2,1)S(1)} %get-tuple-element.26), channel_id=1, source_target_pairs={{0,64},{64,128},{128,192},{192,0},{1,65},{65,129},{129,193},{193,1... | collective-permute-start | bytes 1769480 | tf_op jit(solution)/shard_map/ppermute | solution.py:24
  7.2 25.1 %collective-permute-start = (bf16[4,48,1536]{2,1,0:T(8,128)(2,1)}, bf16[4,48,1536]{2,1,0:T(8,128)(2,1)S(1)}, u32[]{:S(2)}, u32[]{:S(2)}) collective-permute-start(bf16[4,48,1536]{2,1,0:T(8,128)(2,1)} %get-tuple-element.22), channel_id=1, source_target_pairs={{0,16},{16,32},{32,48},{48,0},{1,17},{17,33},{33,49},{49,1},{2,18}... | collective-permute-start | bytes 1769480 | tf_op jit(solution)/shard_map/ppermute | solution.py:24
  8.4 23.9 %collective-permute-start.1 = (bf16[4,48,1536]{2,1,0:T(8,128)(2,1)}, bf16[4,48,1536]{2,1,0:T(8,128)(2,1)}, u32[]{:S(2)}, u32[]{:S(2)}) collective-permute-start(bf16[4,48,1536]{2,1,0:T(8,128)(2,1)} %get-tuple-element.24), channel_id=1, source_target_pairs={{0,48},{16,0},{32,16},{48,32},{1,49},{17,1},{33,17},{49,33},{2,50}... | collective-permute-start | bytes 1769480 | tf_op jit(solution)/shard_map/ppermute | solution.py:24
  9.9 26.4 %collective-permute-start.2 = (bf16[4,48,1536]{2,1,0:T(8,128)(2,1)}, bf16[4,48,1536]{2,1,0:T(8,128)(2,1)}, u32[]{:S(2)}, u32[]{:S(2)}) collective-permute-start(bf16[4,48,1536]{2,1,0:T(8,128)(2,1)} %get-tuple-element.23), channel_id=1, source_target_pairs={{0,32},{16,48},{32,0},{48,16},{1,33},{17,49},{33,1},{49,17},{2,34}... | collective-permute-start | bytes 1769480 | tf_op jit(solution)/shard_map/ppermute | solution.py:24
  11.4 24.8 %collective-permute-start.7 = (bf16[4,48,1536]{2,1,0:T(8,128)(2,1)S(1)}, bf16[4,48,1536]{2,1,0:T(8,128)(2,1)}, u32[]{:S(2)}, u32[]{:S(2)}) collective-permute-start(bf16[4,48,1536]{2,1,0:T(8,128)(2,1)S(1)} %get-tuple-element.25), channel_id=1, source_target_pairs={{0,192},{64,0},{128,64},{192,128},{1,193},{65,1},{129,65},{193,129... | collective-permute-start | bytes 1769480 | tf_op jit(solution)/shard_map/ppermute | solution.py:24
  16.9 19.3 %collective-permute-start.8 = (bf16[4,48,1536]{2,1,0:T(8,128)(2,1)S(1)}, bf16[4,48,1536]{2,1,0:T(8,128)(2,1)}, u32[]{:S(2)}, u32[]{:S(2)}) collective-permute-start(bf16[4,48,1536]{2,1,0:T(8,128)(2,1)S(1)} %get-tuple-element.9), channel_id=1, source_target_pairs={{0,128},{64,192},{128,0},{192,64},{1,129},{65,193},{129,1},{193,65... | collective-permute-start | bytes 1769480 | tf_op jit(solution)/shard_map/ppermute | solution.py:24
  21.4 32.1 %all-to-all-start = ((bf16[16,6,1536]{2,1,0:T(8,128)(2,1)}), bf16[16,6,1536]{2,1,0:T(8,128)(2,1)S(1)}, u32[]{:S(2)}, u32[]{:S(2)}) async-start(bf16[16,6,1536]{2,1,0:T(8,128)(2,1)} %bitcast.59), calls=%async_computation | async-start | bytes 786432 | tf_op jit(solution)/shard_map/all_to_all | solution.py:19
  39.8 20.9 %collective-permute-start.3 = (f32[48,1536]{1,0:T(8,128)}, f32[48,1536]{1,0:T(8,128)}, u32[]{:S(2)}, u32[]{:S(2)}) collective-permute-start(f32[48,1536]{1,0:T(8,128)} %get-tuple-element.28), channel_id=1, source_target_pairs={{0,64},{64,128},{128,192},{192,0},{1,65},{65,129},{129,193},{193,1... | collective-permute-start | bytes 884744 | tf_op jit(solution)/shard_map/ppermute | solution.py:24
  42.8 18.0 %collective-permute-start.4 = (f32[48,1536]{1,0:T(8,128)}, f32[48,1536]{1,0:T(8,128)}, u32[]{:S(2)}, u32[]{:S(2)}) collective-permute-start(f32[48,1536]{1,0:T(8,128)} %get-tuple-element.30), channel_id=1, source_target_pairs={{0,192},{64,0},{128,64},{192,128},{1,193},{65,1},{129,65},{193,129... | collective-permute-start | bytes 884744 | tf_op jit(solution)/shard_map/ppermute | solution.py:24
  43.2 17.5 %collective-permute-start.5 = (f32[48,1536]{1,0:T(8,128)S(1)}, f32[48,1536]{1,0:T(8,128)}, u32[]{:S(2)}, u32[]{:S(2)}) collective-permute-start(f32[48,1536]{1,0:T(8,128)S(1)} %get-tuple-element.29), channel_id=1, source_target_pairs={{0,128},{64,192},{128,0},{192,64},{1,129},{65,193},{129,1},{193,65... | collective-permute-start | bytes 884744 | tf_op jit(solution)/shard_map/ppermute | solution.py:24
  45.3 7.2 %collective-permute-start.9 = (f32[48,1536]{1,0:T(8,128)S(1)}, f32[48,1536]{1,0:T(8,128)S(1)}, u32[]{:S(2)}, u32[]{:S(2)}) collective-permute-start(f32[48,1536]{1,0:T(8,128)S(1)} %get-tuple-element.32), channel_id=1, source_target_pairs={{0,16},{16,32},{32,48},{48,0},{1,17},{17,33},{33,49},{49,1},{2,18}... | collective-permute-start | bytes 884744 | tf_op jit(solution)/shard_map/ppermute | solution.py:24
  45.7 23.5 %collective-permute-start.10 = (f32[48,1536]{1,0:T(8,128)}, f32[48,1536]{1,0:T(8,128)}, u32[]{:S(2)}, u32[]{:S(2)}) collective-permute-start(f32[48,1536]{1,0:T(8,128)} %get-tuple-element.31), channel_id=1, source_target_pairs={{0,48},{16,0},{32,16},{48,32},{1,49},{17,1},{33,17},{49,33},{2,50}... | collective-permute-start | bytes 884744 | tf_op jit(solution)/shard_map/ppermute | solution.py:24
  53.3 16.0 %collective-permute-start.11 = (f32[48,1536]{1,0:T(8,128)S(1)}, f32[48,1536]{1,0:T(8,128)}, u32[]{:S(2)}, u32[]{:S(2)}) collective-permute-start(f32[48,1536]{1,0:T(8,128)S(1)} %get-tuple-element.11), channel_id=1, source_target_pairs={{0,32},{16,48},{32,0},{48,16},{1,33},{17,49},{33,1},{49,17},{2,34}... | collective-permute-start | bytes 884744 | tf_op jit(solution)/shard_map/ppermute | solution.py:24
  54.8 14.2 %all-to-all-start.1 = ((bf16[16,6,1536]{2,1,0:T(8,128)(2,1)}), bf16[16,6,1536]{2,1,0:T(8,128)(2,1)S(1)}, u32[]{:S(2)}, u32[]{:S(2)}) async-start(bf16[16,6,1536]{2,1,0:T(8,128)(2,1)} %gather_fusion), calls=%async_computation.1 | async-start | bytes 786432 | tf_op jit(solution)/shard_map/all_to_all | solution.py:19
  70.6 9.3 %collective-permute-start.13 = (bf16[96,1536]{1,0:T(8,128)(2,1)S(1)}, bf16[96,1536]{1,0:T(8,128)(2,1)S(1)}, u32[]{:S(2)}, u32[]{:S(2)}) collective-permute-start(bf16[96,1536]{1,0:T(8,128)(2,1)S(1)} %fusion.8.refs_0_), channel_id=1, source_target_pairs={{0,14},{2,0},{4,2},{6,4},{8,6},{10,8},{12,10},{14,12},{1,15},{3,1}... | collective-permute-start | bytes 884744 | tf_op jit(solution)/shard_map/ppermute | solution.py:24
  79.9 13.6 %collective-permute-start.15 = (bf16[96,1536]{1,0:T(8,128)(2,1)S(1)}, bf16[96,1536]{1,0:T(8,128)(2,1)S(1)}, u32[]{:S(2)}, u32[]{:S(2)}) collective-permute-start(bf16[96,1536]{1,0:T(8,128)(2,1)S(1)} %collective-permute-done.13.refs_2_), channel_id=1, source_target_pairs={{0,14},{2,0},{4,2},{6,4},{8,6},{10,8},{12,10},{14,12},{1,15},{3,1}... | collective-permute-start | bytes 884744 | tf_op jit(solution)/shard_map/ppermute | solution.py:24
  83.0 13.5 %collective-permute-start.14 = (bf16[96,1536]{1,0:T(8,128)(2,1)S(1)}, bf16[96,1536]{1,0:T(8,128)(2,1)S(1)}, u32[]{:S(2)}, u32[]{:S(2)}) collective-permute-start(bf16[96,1536]{1,0:T(8,128)(2,1)S(1)} %collective-permute-done.12.refs_1_), channel_id=1, source_target_pairs={{0,2},{2,4},{4,6},{6,8},{8,10},{10,12},{12,14},{14,0},{1,3},{3,5},... | collective-permute-start | bytes 884744 | tf_op jit(solution)/shard_map/ppermute | solution.py:24
  83.0 28.3 %collective-permute-start.20 = (bf16[96,1536]{1,0:T(8,128)(2,1)S(1)}, bf16[96,1536]{1,0:T(8,128)(2,1)S(1)}, u32[]{:S(2)}, u32[]{:S(2)}) collective-permute-start(bf16[96,1536]{1,0:T(8,128)(2,1)S(1)} %fusion.8.refs_0_), channel_id=1, source_target_pairs={{0,1},{1,0},{2,3},{3,2},{4,5},{5,4},{6,7},{7,6},{8,9},{9,8},{10,11... | collective-permute-start | bytes 884744 | tf_op jit(solution)/shard_map/ppermute | solution.py:28
  93.5 17.1 %collective-permute-start.17 = (bf16[96,1536]{1,0:T(8,128)(2,1)S(1)}, bf16[96,1536]{1,0:T(8,128)(2,1)S(1)}, u32[]{:S(2)}, u32[]{:S(2)}) collective-permute-start(bf16[96,1536]{1,0:T(8,128)(2,1)S(1)} %collective-permute-done.15.refs_4_), channel_id=1, source_target_pairs={{0,14},{2,0},{4,2},{6,4},{8,6},{10,8},{12,10},{14,12},{1,15},{3,1}... | collective-permute-start | bytes 884744 | tf_op jit(solution)/shard_map/ppermute | solution.py:24
  96.5 10.9 %collective-permute-start.16 = (bf16[96,1536]{1,0:T(8,128)(2,1)S(1)}, bf16[96,1536]{1,0:T(8,128)(2,1)S(1)}, u32[]{:S(2)}, u32[]{:S(2)}) collective-permute-start(bf16[96,1536]{1,0:T(8,128)(2,1)S(1)} %collective-permute-done.14.refs_3_), channel_id=1, source_target_pairs={{0,2},{2,4},{4,6},{6,8},{8,10},{10,12},{12,14},{14,0},{1,3},{3,5},... | collective-permute-start | bytes 884744 | tf_op jit(solution)/shard_map/ppermute | solution.py:24
  97.5 16.6 %all-to-all-start.2 = ((bf16[16,6,1536]{2,1,0:T(8,128)(2,1)}), bf16[16,6,1536]{2,1,0:T(8,128)(2,1)}, u32[]{:S(2)}, u32[]{:S(2)}) async-start(bf16[16,6,1536]{2,1,0:T(8,128)(2,1)} %reshape.67), calls=%async_computation.2 | async-start | bytes 786432 | tf_op jit(solution)/shard_map/all_to_all | solution.py:19
  101.7 14.7 %collective-permute-start.21 = (bf16[96,1536]{1,0:T(8,128)(2,1)S(1)}, bf16[96,1536]{1,0:T(8,128)(2,1)S(1)}, u32[]{:S(2)}, u32[]{:S(2)}) collective-permute-start(bf16[96,1536]{1,0:T(8,128)(2,1)S(1)} %collective-permute-done.12.refs_1_), channel_id=1, source_target_pairs={{0,1},{1,0},{2,3},{3,2},{4,5},{5,4},{6,7},{7,6},{8,9},{9,8},{10,11... | collective-permute-start | bytes 884744 | tf_op jit(solution)/shard_map/ppermute | solution.py:28
  107.3 11.6 %collective-permute-start.22 = (bf16[96,1536]{1,0:T(8,128)(2,1)S(1)}, bf16[96,1536]{1,0:T(8,128)(2,1)S(1)}, u32[]{:S(2)}, u32[]{:S(2)}) collective-permute-start(bf16[96,1536]{1,0:T(8,128)(2,1)S(1)} %collective-permute-done.13.refs_2_), channel_id=1, source_target_pairs={{0,1},{1,0},{2,3},{3,2},{4,5},{5,4},{6,7},{7,6},{8,9},{9,8},{10,11... | collective-permute-start | bytes 884744 | tf_op jit(solution)/shard_map/ppermute | solution.py:28
  107.4 11.6 %collective-permute-start.23 = (bf16[96,1536]{1,0:T(8,128)(2,1)S(1)}, bf16[96,1536]{1,0:T(8,128)(2,1)S(1)}, u32[]{:S(2)}, u32[]{:S(2)}) collective-permute-start(bf16[96,1536]{1,0:T(8,128)(2,1)S(1)} %collective-permute-done.14.refs_3_), channel_id=1, source_target_pairs={{0,1},{1,0},{2,3},{3,2},{4,5},{5,4},{6,7},{7,6},{8,9},{9,8},{10,11... | collective-permute-start | bytes 884744 | tf_op jit(solution)/shard_map/ppermute | solution.py:28
  110.6 8.8 %collective-permute-start.18 = (bf16[48,1536]{1,0:T(8,128)(2,1)}, bf16[48,1536]{1,0:T(8,128)(2,1)}, u32[]{:S(2)}, u32[]{:S(2)}) collective-permute-start(bf16[48,1536]{1,0:T(8,128)(2,1)} %slice.12), channel_id=1, source_target_pairs={{0,2},{2,4},{4,6},{6,8},{8,10},{10,12},{12,14},{14,0},{1,3},{3,5},... | collective-permute-start | bytes 442376 | tf_op jit(solution)/shard_map/ppermute | solution.py:24
  111.3 8.2 %collective-permute-start.19 = (bf16[48,1536]{1,0:T(8,128)(2,1)}, bf16[48,1536]{1,0:T(8,128)(2,1)}, u32[]{:S(2)}, u32[]{:S(2)}) collective-permute-start(bf16[48,1536]{1,0:T(8,128)(2,1)} %slice.13), channel_id=1, source_target_pairs={{0,14},{2,0},{4,2},{6,4},{8,6},{10,8},{12,10},{14,12},{1,15},{3,1}... | collective-permute-start | bytes 442376 | tf_op jit(solution)/shard_map/ppermute | solution.py:24
  116.3 10.1 %collective-permute-start.24 = (bf16[96,1536]{1,0:T(8,128)(2,1)S(1)}, bf16[96,1536]{1,0:T(8,128)(2,1)S(1)}, u32[]{:S(2)}, u32[]{:S(2)}) collective-permute-start(bf16[96,1536]{1,0:T(8,128)(2,1)S(1)} %collective-permute-done.15.refs_4_), channel_id=1, source_target_pairs={{0,1},{1,0},{2,3},{3,2},{4,5},{5,4},{6,7},{7,6},{8,9},{9,8},{10,11... | collective-permute-start | bytes 884744 | tf_op jit(solution)/shard_map/ppermute | solution.py:28
  118.9 7.5 %collective-permute-start.25 = (bf16[96,1536]{1,0:T(8,128)(2,1)S(1)}, bf16[96,1536]{1,0:T(8,128)(2,1)}, u32[]{:S(2)}, u32[]{:S(2)}) collective-permute-start(bf16[96,1536]{1,0:T(8,128)(2,1)S(1)} %collective-permute-done.16.refs_5_), channel_id=1, source_target_pairs={{0,1},{1,0},{2,3},{3,2},{4,5},{5,4},{6,7},{7,6},{8,9},{9,8},{10,11... | collective-permute-start | bytes 884744 | tf_op jit(solution)/shard_map/ppermute | solution.py:28
  119.0 7.5 %collective-permute-start.26 = (bf16[96,1536]{1,0:T(8,128)(2,1)S(1)}, bf16[96,1536]{1,0:T(8,128)(2,1)}, u32[]{:S(2)}, u32[]{:S(2)}) collective-permute-start(bf16[96,1536]{1,0:T(8,128)(2,1)S(1)} %collective-permute-done.17.refs_6_), channel_id=1, source_target_pairs={{0,1},{1,0},{2,3},{3,2},{4,5},{5,4},{6,7},{7,6},{8,9},{9,8},{10,11... | collective-permute-start | bytes 884744 | tf_op jit(solution)/shard_map/ppermute | solution.py:28
  119.5 7.0 %collective-permute-start.27 = (bf16[48,1536]{1,0:T(8,128)(2,1)}, bf16[48,1536]{1,0:T(8,128)(2,1)}, u32[]{:S(2)}, u32[]{:S(2)}) collective-permute-start(bf16[48,1536]{1,0:T(8,128)(2,1)} %collective-permute-done.18.refs_7_), channel_id=1, source_target_pairs={{0,1},{1,0},{2,3},{3,2},{4,5},{5,4},{6,7},{7,6},{8,9},{9,8},{10,11... | collective-permute-start | bytes 442376 | tf_op jit(solution)/shard_map/ppermute | solution.py:28
  119.6 7.0 %collective-permute-start.28 = (bf16[48,1536]{1,0:T(8,128)(2,1)}, bf16[48,1536]{1,0:T(8,128)(2,1)}, u32[]{:S(2)}, u32[]{:S(2)}) collective-permute-start(bf16[48,1536]{1,0:T(8,128)(2,1)} %collective-permute-done.19.refs_8_), channel_id=1, source_target_pairs={{0,1},{1,0},{2,3},{3,2},{4,5},{5,4},{6,7},{7,6},{8,9},{9,8},{10,11... | collective-permute-start | bytes 442376 | tf_op jit(solution)/shard_map/ppermute | solution.py:28
  121.8 44.2 %all-to-all-start.3 = ((bf16[16,6,1536]{2,1,0:T(8,128)(2,1)}), bf16[16,6,1536]{2,1,0:T(8,128)(2,1)}, u32[]{:S(2)}, u32[]{:S(2)}) async-start(bf16[16,6,1536]{2,1,0:T(8,128)(2,1)} %broadcast_select_fusion), calls=%async_computation.3 | async-start | bytes 786432 | tf_op jit(solution)/shard_map/all_to_all | solution.py:19
  (5 other events, 33.2 us)
